TPU v7x, 128 devices: a whole 4x4x4 slice. The times are simulated.
128 devices in a mesh: row: 8 (over x_hi, z), col: 16 (over x_lo, y, core).
Axes of the slice: x: 4 (x_hi: 2, x_lo: 2; x = x_hi * 2 + x_lo), y: 4, z: 4, core: 2. Of those that a mesh axis runs over, the one named last changes fastest.
Arguments:
- density_cyclic: float32 [6144, 6144], P(('row', 'col')), as said below
- mask_in: int32 [48, 48], replicated, may hold values from 0 to 1, as said below
- mask_sq: int32 [48, 48], replicated, may hold values from 0 to 1, as said below
- mask_cube: int32 [48, 48], replicated, may hold values from 0 to 1, as said below
Outputs:
- purified: float32 [6144, 6144], P('row', 'col')
- trace: float32 [], replicated
Inputs may be any that keep to these rules, and one draw needn't show every extreme that they name: `density_cyclic`: density, the matrix with its rows in order, is symmetric. `mask_in`: symmetric, with ones on the diagonal. `mask_sq`: symmetric, with ones on the diagonal. `mask_cube`: symmetric, with ones on the diagonal.
All inputs are finite; a program needn't handle non-finite values.
Results may differ from a plain program's by a relative error of at most 0.00009.
Values sent between devices are 32-bit elements; how exact they have to be, the bound alone decides.
A program may use at most 128 MiB of HBM per device.

v0:
```python
import jax
import jax.numpy as jnp
from jax import lax
from jax.sharding import PartitionSpec as P

BS = 128


def local_mask(mask, top, left, rows, cols):
    piece = lax.dynamic_slice(mask, (top, left), (rows // BS, cols // BS)).astype(jnp.float32)
    return piece[:, None, :, None]


def apply_mask(block, piece):
    rows, cols = block.shape
    shaped = block.reshape(piece.shape[0], BS, piece.shape[2], BS) * piece
    return shaped.reshape(rows, cols)


def fold_rows(panel, piece):
    return jnp.dot(
        panel, piece, precision=lax.Precision.HIGHEST, preferred_element_type=jnp.float32
    )


def shards(density_cyclic, mask_in, mask_sq, mask_cube):
    nrow = lax.axis_size("row")
    ncol = lax.axis_size("col")
    devices = nrow * ncol
    order = density_cyclic.shape[1]
    stored = density_cyclic.shape[0]
    per_group = stored // nrow
    rows = order // nrow
    cols = order // ncol
    outgoing = density_cyclic.reshape(nrow, per_group, ncol, cols).transpose(0, 2, 1, 3)
    outgoing = outgoing.reshape(devices, per_group, cols)
    incoming = lax.all_to_all(outgoing, ("row", "col"), split_axis=0, concat_axis=0, tiled=True)
    block = incoming.transpose(1, 0, 2).reshape(rows, cols)
    row_index = lax.axis_index("row")
    col_index = lax.axis_index("col")
    top = row_index * (rows // BS)
    left = col_index * (cols // BS)
    filtered = apply_mask(block, local_mask(mask_in, top, left, rows, cols))
    row_slab = lax.all_gather(filtered, "col", axis=1, tiled=True)
    square = fold_rows(row_slab, lax.all_gather(filtered, "row", axis=0, tiled=True))
    square = apply_mask(square, local_mask(mask_sq, top, left, rows, cols))
    square_slab = lax.all_gather(square, "col", axis=1, tiled=True)
    cube = fold_rows(square_slab, lax.all_gather(filtered, "row", axis=0, tiled=True))
    cube = apply_mask(cube, local_mask(mask_cube, top, left, rows, cols))
    purified = 3.0 * square - 2.0 * cube
    global_rows = row_index * rows + lax.iota(jnp.int32, rows)
    global_cols = col_index * cols + lax.iota(jnp.int32, cols)
    diagonal = global_rows[:, None] == global_cols[None, :]
    partial_trace = jnp.sum(jnp.where(diagonal, purified, jnp.float32(0.0)))
    total = lax.psum(partial_trace, ("row", "col"))
    return (purified, total)


def solution(mesh):
    in_specs = (P(("row", "col"), None), P(), P(), P())
    out_specs = (P("row", "col"), P())
    return jax.shard_map(shards, mesh=mesh, in_specs=in_specs, out_specs=out_specs, check_vma=False)
```

profile of v0, /device:TPU:8, one launch (start us, length us, event | category | flops | bytes accessed | tf_op | source)
XLA Modules:
  0.0 505.2 jit_solution(4865591503840753998)
XLA Ops:
  7.2 1.5 copy.28
  8.6 0.1 copy.19
  8.8 1.9 copy.20
  10.6 10.4 %all-to-all-start = ((f32[128,6,384]{2,1,0:T(8,128)}), f32[128,6,384]{2,1,0:T(8,128)S(1)}, u32[]{:S(2)}, u32[]{:S(2)}) async-start(f32[128,6,384]{2,1,0:T(8,128)} %copy.20), calls=%async_computation | async-start | bytes 3145728 | tf_op jit(solution)/shard_map/all_to_all | solution.py:37
  21.1 0.0 all-gather.6.cloned.1.call-start
  21.1 0.8 dynamic-slice_convert_fusion.2
  21.9 0.1 copy.22
  22.0 0.2 mul.59
  22.2 1.3 copy.37
  23.4 1.6 copy.23
  25.1 20.2 %all-to-all-done = f32[128,6,384]{2,1,0:T(8,128)S(1)} async-done(((f32[128,6,384]{2,1,0:T(8,128)}), f32[128,6,384]{2,1,0:T(8,128)S(1)}, u32[]{:S(2)}, u32[]{:S(2)}) %all-to-all-start) | async-done | bytes 1179680 | tf_op jit(solution)/shard_map/all_to_all | solution.py:37
  45.3 0.2 copy.21
  45.5 1.1 bitcast_multiply_fusion
  46.6 0.0 all-gather.6.cloned.1.call-update
  46.6 0.0 all-gather.4.cloned.1.call-start
  46.7 0.7 all-gather.4.cloned.1.call-update
  47.4 0.0 all-gather.8.cloned.1.call-start
  47.4 0.8 dynamic-slice_convert_fusion
  48.2 0.1 copy.24
  48.3 0.2 mul.62
  48.5 0.3 copy.36
  48.8 0.4 copy.25
  49.2 110.8 %all-gather.6.cloned.1.call-done = f32[6144,384]{1,0:T(8,128)} async-done(((f32[768,384]{1,0:T(8,128)}), f32[6144,384]{1,0:T(8,128)}) %all-gather.6.cloned.1.call-update) | async-done | bytes 9437200 | tf_op jit(solution)/shard_map/all_gather | solution.py:45
  160.0 101.5 %all-gather.4.cloned.1.call-done = f32[768,6144]{1,0:T(8,128)} async-done(((f32[768,384]{1,0:T(8,128)}), f32[768,6144]{1,0:T(8,128)}) %all-gather.4.cloned.1.call-update) | async-done | bytes 18874384 | tf_op jit(solution)/shard_map/all_gather | solution.py:44
  261.5 34.2 %convolution_multiply_fusion.1 = f32[768,384]{1,0:T(8,128)} fusion(f32[768,384]{1,0:T(8,128)S(1)} %copy.25, f32[768,6144]{1,0:T(8,128)} %all-gather.4.cloned.1.call-done, f32[6144,384]{1,0:T(8,128)} %all-gather.6.cloned.1.call-done), kind=kOutput, calls=%fused_computation.1 | convolution fusion | flops 21743566848 | bytes 30670848 | tf_op jit(solution)/shard_map/dot_general | solution.py:21
  295.7 0.1 copy.26
  295.8 0.2 mul.67
  295.9 0.3 copy.35
  296.2 0.4 copy.27
  296.6 101.6 %all-gather.8.cloned.1.call-done = f32[768,6144]{1,0:T(8,128)} async-done(((f32[768,384]{1,0:T(8,128)}), f32[768,6144]{1,0:T(8,128)}) %all-gather.8.cloned.1.call-update) | async-done | bytes 18874384 | tf_op jit(solution)/shard_map/all_gather | solution.py:47
  398.2 35.1 %select_reduce_fusion = (f32[]{:T(128)}, f32[768,384]{1,0:T(8,128)}) fusion(s32[384]{0:T(512)S(1)} %iota_add_fusion.1, s32[768]{0:T(1024)S(1)} %iota_add_fusion, f32[768,384]{1,0:T(8,128)S(1)} %copy.27, f32[768,6144]{1,0:T(8,128)} %all-gather.8.cloned.1.call-done, f32[6144,384]{1,0:T(8,128)} %all-gather.6.cloned.1.call-done, f32[768,384]{1,0:T(8,128)S(1)} %copy-done), kind=kOutput, calls=%fused_computation.8 | convolution fusion | flops 21745336320 | bytes 31855108 | tf_op jit(solution)/shard_map/dot_general | solution.py:21
  433.3 65.4 %psum.7 = f32[]{:T(128)} all-reduce(f32[]{:T(128)} %get-tuple-element.2), channel_id=1, replica_groups=mesh['row'=8,'col'=16] {'row','col'}, use_global_device_ids=true, to_apply=%region_1.2 | all-reduce | flops 1 | bytes 8 | tf_op jit(solution)/shard_map/psum | solution.py:55
  (5 shorter events, 0.0 us)
Async XLA Ops:
  10.6 34.6 %all-to-all-start = ((f32[128,6,384]{2,1,0:T(8,128)}), f32[128,6,384]{2,1,0:T(8,128)S(1)}, u32[]{:S(2)}, u32[]{:S(2)}) async-start(f32[128,6,384]{2,1,0:T(8,128)} %copy.20), calls=%async_computation | async-start | bytes 3145728 | tf_op jit(solution)/shard_map/all_to_all | solution.py:37
  21.1 138.9 %all-gather.6.cloned.1.call-start = ((), (), s32[]{:S(2)}) async-start(), calls=%async_computation.2 | async-start | bytes 10616832 | tf_op jit(solution)/shard_map/all_gather | solution.py:45
  46.6 214.8 %all-gather.4.cloned.1.call-start = ((), (), s32[]{:S(2)}) async-start(), calls=%async_computation.1 | async-start | bytes 20054016 | tf_op jit(solution)/shard_map/all_gather | solution.py:44
  47.4 350.8 %all-gather.8.cloned.1.call-start = ((), (), s32[]{:S(2)}) async-start(), calls=%async_computation.3 | async-start | bytes 20054016 | tf_op jit(solution)/shard_map/all_gather | solution.py:47
  296.2 102.0 %copy-start = (f32[768,384]{1,0:T(8,128)S(1)}, f32[768,384]{1,0:T(8,128)}, u32[]{:S(2)}) copy-start(f32[768,384]{1,0:T(8,128)} %convolution_multiply_fusion.1) | copy-start | bytes 3538948
Sparse Core Ops, SparseCore 0:
  46.8 113.1 all-gather.5
  162.2 99.1 all-gather.3
  295.8 102.4 all-gather.7
where the time goes:
time: 507 us; the launch traced here: 505 us
  waiting for transfers between devices  335 us (66%)
  matrix products  69.2 us (14%)
  blocking collectives  65.4 us (13%)
  between operations  13.9 us (3%)
  starting transfers between devices  10.6 us (2%)
  local copies, waits for them, and re-layouts  8.61 us (2%)
    all_gather x1, waiting for transfers between devices, shards(): lax.all_gather(filtered, 'row', axis=0, tiled=True)  111 us
    all_gather x1, waiting for transfers between devices, shards(): square_slab = lax.all_gather(square, 'col', axis=1, tiled=True)  102 us
    all_gather x1, waiting for transfers between devices, shards(): row_slab = lax.all_gather(filtered, 'col', axis=1, tiled=True)  101 us
    dot_general x2, matrix products, fold_rows(): jnp.dot(panel, piece, precision=lax.Precision.HIGHEST, preferred_element_...  69.2 us
    psum x1, blocking collectives, shards(): total = lax.psum(partial_trace, ('row', 'col'))  65.4 us
    all_to_all x1, waiting for transfers between devices, shards(): lax.all_to_all(outgoing, ('row', 'col'), split_axis=0, concat_axis=0, til...  20.2 us
    all_to_all x1, starting transfers between devices, shards(): lax.all_to_all(outgoing, ('row', 'col'), split_axis=0, concat_axis=0, til...  10.4 us
  transfers between devices with their start and end apart: 4, of which 4 were waited for; matrix products, arithmetic and copies ran while one was open for 1% of the time, Pallas kernels for 0%

commit v1 on v0

v1 whole, which is shorter than its diff:
```python
import functools

import jax
import jax.numpy as jnp
from jax import lax
from jax.experimental import pallas as pl
from jax.experimental.pallas import tpu as pltpu
from jax.sharding import PartitionSpec as P

F32 = jnp.float32
BF16 = jnp.bfloat16
MESH = pl.DeviceIdType.MESH
BS = 128
NB = 48
HALF = 3072
KC = 4
RC = 4
ROWS = 768 // RC


def split(x):
    hi = x.astype(BF16)
    return hi, (x - hi.astype(F32)).astype(BF16)


def dot(a, b):
    return jnp.dot(a, b, preferred_element_type=F32)


def dot3(a, bh, bl):
    ah, al = split(a)
    return dot(ah, bh) + (dot(al, bh) + dot(ah, bl))


def kernel(
    t1src, t2src, msq, mcu, mdg, tr0, out, trace,
    t1recv, t2recv, acol, lhs, bhi, blo, sacc, rs1, sfull, cacc, rs2, order, tsend, trecv,
    ss, rs, ls,
):
    row = lax.axis_index("row")
    col = lax.axis_index("col")
    xh, z = row // 4, row % 4
    xl, y, c = col // 8, (col // 2) % 4, col % 2
    piece = col % 8

    def at(xh_=xh, xl_=xl, y_=y, z_=z, c_=c):
        return (xh_ * 4 + z_, (xl_ * 4 + y_) * 2 + c_)

    zp, zm, z2 = (z + 1) % 4, (z + 3) % 4, (z + 2) % 4
    yp, ym, y2 = (y + 1) % 4, (y + 3) % 4, (y + 2) % 4
    ox, ol, oc = 1 - xh, 1 - xl, 1 - c

    group1 = [
        ((xl + a) % 2, (y + b) % 4, (c + e) % 2)
        for b in (0, 1, 3, 2) for a in range(2) for e in range(2) if (a, b, e) != (0, 0, 0)
    ]
    group2 = [
        ((xh + a) % 2, (xl + b) % 2, (z + e) % 4)
        for e in (0, 1, 3, 2) for a in range(2) for b in range(2) if (a, b, e) != (0, 0, 0)
    ]
    partners = [at(xl_=a, y_=b, c_=e) for a, b, e in group1]
    partners += [at(xh_=a, xl_=b, z_=e) for i, (a, b, e) in enumerate(group2) if i != 0]

    barrier = pltpu.get_barrier_semaphore()
    for dev in partners:
        pl.semaphore_signal(barrier, inc=1, device_id=dev, device_id_type=MESH)
    pl.semaphore_wait(barrier, len(partners))

    copies = []

    def send(src, dst, dev):
        i = len(copies)
        copy = pltpu.make_async_remote_copy(
            src_ref=src, dst_ref=dst, send_sem=ss.at[i], recv_sem=rs.at[i], device_id=dev, device_id_type=MESH
        )
        copy.start()
        copies.append(copy)
        return copy

    slot1 = pl.ds(pl.multiple_of(col * 144, 8), 144)
    slot2 = pl.ds(pl.multiple_of((row * 2 + xl) * 144, 8), 144)
    own1 = pltpu.make_async_copy(t1src.at[xl, y, c], t1recv.at[slot1], ls.at[0])
    own1.start()
    own2 = pltpu.make_async_copy(t2src.at[xl, row], t2recv.at[slot2], ls.at[1])
    own2.start()
    a1, a2 = [], []
    for (a, b, e), (f, g, h) in zip(group1, group2):
        a1.append(send(t1src.at[a, b, e], t1recv.at[slot1], at(xl_=a, y_=b, c_=e)))
        a2.append(send(t2src.at[g, f * 4 + h], t2recv.at[slot2], at(xh_=f, xl_=g, z_=h)))
    own1.wait()
    for copy in a1:
        copy.wait_recv()

    def order1(blk, carry):
        for g in range(2):
            for j in range(6):
                lanes = pl.ds(j * 128, 128)
                acol[blk, row, pl.ds(g * 8, 8), lanes] = t1recv[pl.ds(g * 8 * 144 + blk * 6 + j, 8, stride=144), :]
        return carry

    lax.fori_loop(0, 24, order1, 0)

    def cols(n, slot, first=0, count=6):
        return acol.at[pl.ds(n * 6 + first, count), slot]

    def rows(n, slot):
        return lhs.at[slot, :, pl.ds(n * 768, 768)]

    g1 = [{} for _ in range(KC)]
    g2 = [{} for _ in range(KC)]

    def start1(n):
        ref = cols(n, row)
        g1[n]["x"] = send(ref, ref, at(xh_=ox))
        g1[n]["zp"] = send(ref, ref, at(z_=zp))
        g1[n]["zm"] = send(ref, ref, at(z_=zm))

    def relay1(n):
        g1[n]["x"].wait_recv()
        ref = cols(n, ox * 4 + z)
        g1[n]["qp"] = send(ref, ref, at(z_=zp))
        g1[n]["qm"] = send(ref, ref, at(z_=zm))
        g1[n]["zp"].wait_recv()
        ref = cols(n, xh * 4 + zm, 0, 3)
        g1[n]["hp"] = send(ref, ref, at(z_=zp))
        g1[n]["zm"].wait_recv()
        ref = cols(n, xh * 4 + zp, 3, 3)
        g1[n]["hm"] = send(ref, ref, at(z_=zm))

    def cross1(n):
        g1[n]["hp"].wait_recv()
        ref = cols(n, xh * 4 + z2, 0, 3)
        g1[n]["xp"] = send(ref, ref, at(xh_=ox))
        g1[n]["hm"].wait_recv()
        ref = cols(n, xh * 4 + z2, 3, 3)
        g1[n]["xm"] = send(ref, ref, at(xh_=ox))

    def end1(n):
        for key in ("qp", "qm", "xp", "xm"):
            g1[n][key].wait_recv()

    def start2(n):
        ref = rows(n, piece)
        g2[n]["c"] = send(ref, ref, at(c_=oc))
        g2[n]["yp"] = send(ref, ref, at(y_=yp))
        g2[n]["ym"] = send(ref, ref, at(y_=ym))
        g2[n]["y2"] = send(ref, ref, at(y_=y2))

    def relay2(n):
        for key, other in (("yp", ym), ("ym", yp), ("y2", y2)):
            g2[n][key].wait_recv()
            ref = rows(n, other * 2 + c)
            g2[n]["c" + key] = send(ref, ref, at(c_=oc))

    def end2(n):
        for key in ("c", "cyp", "cym", "cy2"):
            g2[n][key].wait_recv()

    start1(0)
    start1(1)
    own2.wait()
    for copy in a2:
        copy.wait_recv()

    def order2(blk, carry):
        for g in range(2):
            for j in range(24):
                start = g * 8 * 144 + blk * 24 + j
                lhs[piece, pl.ds(pl.multiple_of(blk * 16 + g * 8, 8), 8), pl.ds(j * 128, 128)] = t2recv[
                    pl.ds(start, 8, stride=144), :
                ]
        return carry

    lax.fori_loop(0, 6, order2, 0)
    start2(0)
    start2(1)

    def prepare(n):
        def body(b, carry):
            hi, lo = split(acol[n * 6 + b].reshape(BS, 768))
            at_ = pl.ds(pl.multiple_of(n * 768 + b * BS, BS), BS)
            bhi[at_, :] = hi
            blo[at_, :] = lo
            return carry

        lax.fori_loop(0, 6, body, 0)

    def square_rows(n, r):
        a = lhs[pl.ds(r * 2, 2), :, pl.ds(n * 768, 768)].reshape(ROWS, 768)
        k = pl.ds(n * 768, 768)
        got = dot3(a, bhi[k, :], blo[k, :])
        m = pl.ds(pl.multiple_of(r * ROWS, ROWS), ROWS)
        sacc[m, :] = got if n == 0 else sacc[m, :] + got

    s1 = []

    def square(n):
        prepare(n)
        if n < KC - 1:
            def body(r, carry):
                square_rows(n, r)
                return carry

            lax.fori_loop(0, RC, body, 0)
        else:
            for r in range(RC):
                square_rows(n, r)
                m = pl.ds(r * ROWS, ROWS)
                s1.append(send(sacc.at[m, pl.ds(384, 384)], rs1.at[m], at(xl_=ol)))

    for t in range(KC + 2):
        if t < KC:
            relay1(t)
            if t + 2 < KC:
                start1(t + 2)
            relay2(t)
            if t + 2 < KC:
                start2(t + 2)
        if 0 <= t - 1 < KC:
            cross1(t - 1)
        if 0 <= t - 2 < KC:
            end1(t - 2)
            end2(t - 2)
            square(t - 2)

    mine = pl.multiple_of(piece * 384, 128)
    g3 = [{} for _ in range(RC)]
    s2 = [None] * RC
    total = [tr0[...]]

    def begin3(r):
        m = pl.ds(r * ROWS, ROWS)
        s1[r].wait_recv()
        s = (sacc[m, pl.ds(0, 384)] + rs1[m, :]).reshape(2, 6, 16, 384) * msq[...][None]
        sfull[piece, m, :] = s.reshape(ROWS, 384)
        ref = sfull.at[piece, m]
        g3[r]["yp"] = send(ref, ref, at(y_=yp))
        g3[r]["ym"] = send(ref, ref, at(y_=ym))
        g3[r]["c"] = send(ref, ref, at(c_=oc))
        a = lhs[pl.ds(r * 2, 2), :, pl.ds(mine, 384)].reshape(2, 6, 16, 384)
        part = jnp.sum((s * a * mdg[...][None]).reshape(24, 8, 384), axis=0)
        total[0] = total[0] - 2.0 * (part[:, 0:128] + part[:, 128:256] + part[:, 256:384])

    def relay3(r):
        m = pl.ds(r * ROWS, ROWS)
        g3[r]["yp"].wait_recv()
        ref = sfull.at[ym * 2 + c, pl.ds(r * ROWS, ROWS // 2)]
        g3[r]["hp"] = send(ref, ref, at(y_=yp))
        ref = sfull.at[ym * 2 + c, m]
        g3[r]["cyp"] = send(ref, ref, at(c_=oc))
        g3[r]["ym"].wait_recv()
        ref = sfull.at[yp * 2 + c, pl.ds(r * ROWS + ROWS // 2, ROWS // 2)]
        g3[r]["hm"] = send(ref, ref, at(y_=ym))
        ref = sfull.at[yp * 2 + c, m]
        g3[r]["cym"] = send(ref, ref, at(c_=oc))

    def far3(r):
        g3[r]["hp"].wait_recv()
        ref = sfull.at[y2 * 2 + c, pl.ds(r * ROWS, ROWS // 2)]
        g3[r]["chp"] = send(ref, ref, at(c_=oc))
        g3[r]["hm"].wait_recv()
        ref = sfull.at[y2 * 2 + c, pl.ds(r * ROWS + ROWS // 2, ROWS // 2)]
        g3[r]["chm"] = send(ref, ref, at(c_=oc))

    def cube(r):
        m = pl.ds(r * ROWS, ROWS)
        for key in ("c", "cyp", "cym", "chp", "chm"):
            g3[r][key].wait_recv()

        def body(s, carry):
            k = pl.ds(pl.multiple_of(s * 384, 384), 384)
            cacc[m, :] = cacc[m, :] + dot3(sfull[s, m, :], bhi[k, :], blo[k, :])
            return carry

        cacc[m, :] = jnp.zeros((ROWS, 768), F32)
        lax.fori_loop(0, 8, body, 0)
        s2[r] = send(cacc.at[m, pl.ds(384, 384)], rs2.at[m], at(xl_=ol))

    def finish(r):
        m = pl.ds(r * ROWS, ROWS)
        s2[r].wait_recv()
        got = (cacc[m, pl.ds(0, 384)] + rs2[m, :]).reshape(2, 6, 16, 384) * mcu[...][None]
        got = 3.0 * sfull[piece, m, :] - 2.0 * got.reshape(ROWS, 384)
        for i in range(2):
            for j in range(3):
                order[pl.ds(j * 768 + r * 2 + i, 96, stride=8), :] = got[
                    i * 96:(i + 1) * 96, j * 128:(j + 1) * 128
                ]

    steps = [at(c_=oc), at(xl_=ol), at(xh_=ox), at(y_=y + 1 - 2 * (y % 2)), at(z_=z + 1 - 2 * (z % 2)), at(y_=y2), at(z_=z2)]
    flying = []

    def trace_step():
        if flying:
            n, copy = flying.pop()
            copy.wait_recv()
            total[0] = total[0] + trecv[n]
            if n + 1 == len(steps):
                trace[...] = total[0]
                return
            n = n + 1
        else:
            n = 0
        if n >= len(steps):
            return
        tsend[n] = total[0]
        flying.append((n, send(tsend.at[n], trecv.at[n], steps[n])))

    left = len(steps) + 1

    def advance(t):
        nonlocal left
        if t >= RC and left:
            trace_step()
            left -= 1

    for t in range(RC + 4):
        if t < RC:
            begin3(t)
        advance(t)
        if 0 <= t - 1 < RC:
            relay3(t - 1)
            advance(t)
        if 0 <= t - 2 < RC:
            far3(t - 2)
            advance(t)
        if 0 <= t - 3 < RC:
            cube(t - 3)
            advance(t)
        if 0 <= t - 4 < RC:
            finish(t - 4)
    for j in range(3):
        out[:, pl.ds(j * 128, 128)] = order[pl.ds(j * 768, 768), :]
    while left:
        trace_step()
        left -= 1
    assert len(copies) == N_COPIES
    for copy in copies:
        copy.wait_send()


N_COPIES = 30 + KC * 16 + RC * 11 + 7


def call(t1src, t2src, msq, mcu, mdg, tr0):
    vmem = pl.BlockSpec(memory_space=pltpu.VMEM)
    hbm = pl.BlockSpec(memory_space=pl.ANY)
    return pl.pallas_call(
        kernel,
        out_shape=(jax.ShapeDtypeStruct((768, 384), F32), jax.ShapeDtypeStruct((8, 128), F32)),
        in_specs=[hbm, hbm, vmem, vmem, vmem, vmem],
        out_specs=(vmem, vmem),
        scratch_shapes=[
            pltpu.VMEM((2304, 128), F32),
            pltpu.VMEM((2304, 128), F32),
            pltpu.VMEM((24, 8, 16, 768), F32),
            pltpu.VMEM((8, 96, HALF), F32),
            pltpu.VMEM((HALF, 768), BF16),
            pltpu.VMEM((HALF, 768), BF16),
            pltpu.VMEM((768, 768), F32),
            pltpu.VMEM((768, 384), F32),
            pltpu.VMEM((8, 768, 384), F32),
            pltpu.VMEM((768, 768), F32),
            pltpu.VMEM((768, 384), F32),
            pltpu.VMEM((2304, 128), F32),
            pltpu.VMEM((7, 8, 128), F32),
            pltpu.VMEM((7, 8, 128), F32),
            pltpu.SemaphoreType.DMA((N_COPIES,)),
            pltpu.SemaphoreType.DMA((N_COPIES,)),
            pltpu.SemaphoreType.DMA((2,)),
        ],
        compiler_params=pltpu.CompilerParams(
            collective_id=0, has_side_effects=True, vmem_limit_bytes=62 * 2**20
        ),
        cost_estimate=pl.CostEstimate(flops=2 * 768 * 768 * HALF * 6, bytes_accessed=4 * 2**20, transcendentals=0),
    )(t1src, t2src, msq, mcu, mdg, tr0)


def shards(density_cyclic, mask_in, mask_sq, mask_cube):
    row = lax.axis_index("row")
    col = lax.axis_index("col")
    pm = density_cyclic.reshape(NB, NB, BS) * mask_in.astype(F32)[:, :, None]
    t2src = pm.reshape(8, 6, 2, 24, BS).transpose(2, 0, 1, 3, 4).reshape(2, 8, 144, BS)
    both = pm.reshape(2, 24, 2, 4, 2, 384)
    both = jnp.stack([both[0], both[1][:, ::-1]])
    t1src = both.transpose(0, 3, 4, 1, 2, 5).reshape(2, 4, 2, 144, BS)

    def tile(mask):
        piece = lax.dynamic_slice(mask, (row * 6, col * 3), (6, 3)).astype(F32)
        return jnp.broadcast_to(piece[:, None, :, None], (6, 16, 3, BS)).reshape(6, 16, 384)

    mdiag = lax.dynamic_slice(jnp.diagonal(mask_cube), (row * 6,), (6,)).astype(F32)
    mdg = jnp.broadcast_to(mdiag[:, None, None], (6, 16, 384))
    weight = jnp.diagonal(mask_sq).astype(F32)[:, None, None]
    tr0 = 3.0 * jnp.sum((pm * pm * weight).reshape(NB * 6, 8, BS), axis=0)
    purified, trace = call(t1src, t2src, tile(mask_sq), tile(mask_cube), mdg, tr0)
    return purified, jnp.sum(trace)


def solution(mesh):
    in_specs = (P(("row", "col"), None), P(), P(), P())
    out_specs = (P("row", "col"), P())
    return jax.shard_map(shards, mesh=mesh, in_specs=in_specs, out_specs=out_specs, check_vma=False)
```

time: 507 us -> 219 us (0.43)
  waiting for transfers between devices: 335 us -> 0 us
  Pallas kernels: 0 us -> 194 us
  matrix products: 69.2 us -> 0 us
  blocking collectives: 65.4 us -> 0 us
  between operations: 13.9 us -> 0.75 us
  starting transfers between devices: 10.6 us -> 0 us
  local copies, waits for them, and re-layouts: 8.61 us -> 16.3 us
  other arithmetic: 2.73 us -> 8.1 us
    all_gather x3 -> x0, waiting for transfers between devices: 314 us -> none  [the longest x1 111 us: shards(): lax.all_gather(filtered, 'row', axis=0, tiled=True)]
    pallas_call x0 -> x1, Pallas kernels: none -> 194 us  [call(): pl.pallas_call(kernel, out_shape=(jax.ShapeDtypeStruct((768, 384), F32),...]
    dot_general x2 -> x0, matrix products: 69.2 us -> none  [fold_rows(): jnp.dot(panel, piece, precision=lax.Precision.HIGHEST, preferred_element_...]
    psum x1 -> x0, blocking collectives: 65.4 us -> none  [shards(): total = lax.psum(partial_trace, ('row', 'col'))]
    all_to_all x1 -> x0, waiting for transfers between devices: 20.2 us -> none  [shards(): lax.all_to_all(outgoing, ('row', 'col'), split_axis=0, concat_axis=0, til...]
    all_to_all x1 -> x0, starting transfers between devices: 10.4 us -> none  [shards(): lax.all_to_all(outgoing, ('row', 'col'), split_axis=0, concat_axis=0, til...]
  transfers between devices with their start and end apart: 4 -> 0, of which waited for: 4 -> 0; matrix products, arithmetic and copies ran while one was open for 1% -> 0% of each run, Pallas kernels for 0% -> 0%
where the time goes in v1:
time: 219 us
  Pallas kernels  194 us (89%)
  local copies, waits for them, and re-layouts  16.3 us (7%)
  other arithmetic  8.1 us (4%)
    pallas_call x1, Pallas kernels, call(): pl.pallas_call(kernel, out_shape=(jax.ShapeDtypeStruct((768, 384), F32),...  194 us

profile of v1, /device:TPU:8, one launch (start us, length us, event | category | flops | bytes accessed | tf_op | source)
XLA Modules:
  0.0 218.9 jit_solution(3656135200829919690)
XLA Ops:
  0.6 0.9 dynamic-slice_convert_fusion
  1.5 0.1 broadcast_bitcast_fusion.1
  1.6 0.7 broadcast_in_dim.36.msq
  2.3 0.1 broadcast_bitcast_fusion
  2.4 0.7 broadcast_in_dim.39.mcu
  3.0 1.7 gather_fusion
  4.8 0.1 dynamic-slice_convert_fusion.2
  4.9 0.8 broadcast_in_dim.40.mdg
  5.6 0.7 convert_element_type.19
  6.4 0.2 copy.11
  6.6 0.4 copy-done.3
  7.0 0.4 bitcast_multiply_fusion
  7.3 0.9 fusion
  8.2 1.4 squeeze.3
  9.6 1.0 reverse_bitcast_fusion
  10.7 1.1 slice.11
  11.8 1.6 maximum_bitcast_fusion
  13.4 0.6 copy.8
  14.0 2.0 reshape.40.t1src
  16.0 0.8 mul.56
  16.9 0.0 copy-start
  16.9 1.4 copy_multiply_fusion
  18.3 0.1 mul.61
  18.4 1.0 gather_fusion.1
  19.4 0.1 mul.65
  19.4 0.1 mul.66
  19.6 0.2 reshape.43
  19.7 1.1 multiply_reduce_fusion
  20.9 0.6 broadcast_multiply_fusion.tr0
  21.5 193.8 %shard_map.59 = (f32[768,384]{1,0:T(8,128)}, f32[8,128]{1,0:T(8,128)}) custom-call(f32[2,4,2,144,128]{4,3,2,1,0:T(8,128)} %reshape.40.t1src, f32[2,8,144,128]{3,2,1,0:T(8,128)} %bitcast.27, f32[6,16,384]{2,1,0:T(8,128)} %broadcast_in_dim.36.msq, f32[6,16,384]{2,1,0:T(8,128)} %broadcast_in_dim.39.mcu, f32[6,16,384]{2,1,0:T(8,128)} %broadcast_in_dim.40.mdg, ...), custom_call_target="tpu_custom_call" | custom-call | flops 21743271936 | bytes 4194304 | tf_op jit(solution)/shard_map/pallas_call | solution.py:348
  215.3 1.3 reduce_sum.19
  216.6 2.4 %copy.21 = f32[768,384]{1,0:T(8,128)} copy(f32[768,384]{1,0:T(8,128)} %get-tuple-element.12) | data formatting | bytes 2359296
  (13 shorter events, 0.1 us)
Async XLA Ops:
  0.6 5.7 %copy-start.1 = (f32[48,6144]{1,0:T(8,128)S(1)}, f32[48,6144]{1,0:T(8,128)}, u32[]{:S(2)}) copy-start(f32[48,6144]{1,0:T(8,128)} %param.4) | copy-start | bytes 3538948
  6.3 0.6 copy-start.3
  10.7 1.2 copy-start.2
  16.9 1.4 copy-start.4
  16.9 1.5 copy-start

commit v2 on v0

v2 whole, which is shorter than its diff:
```python
import jax
import jax.numpy as jnp
from jax import lax
from jax.experimental import pallas as pl
from jax.experimental.pallas import tpu as pltpu
from jax.sharding import PartitionSpec as P

F32 = jnp.float32
BF16 = jnp.bfloat16
MESH = pl.DeviceIdType.MESH
BS = 128
NB = 48
HALF = 3072
OWN, OTHER = 0, 1
CHUNKS = ((OTHER, 0, "x"), (OTHER, 1, "x"), (OWN, 0, "z"), (OWN, 1, "z"))
RC = 8
ROWS = 768 // RC
PIECES = 8 // RC


def split(x):
    hi = x.astype(BF16)
    return hi, (x - hi.astype(F32)).astype(BF16)


def dot(a, b):
    return jnp.dot(a, b, preferred_element_type=F32)


def dot3(a, bh, bl):
    ah, al = split(a)
    return dot(ah, bh) + (dot(al, bh) + dot(ah, bl))


def kernel(
    den, mask_in, mask_sq, mask_cube, out, trace,
    local, t1recv, t2src, t2mid, t2recv, flat, acol, lhs, bhi, blo, so, sw, rs1, sfull, cacc, rs2, tacc, tone, ttwo,
    ss, rs, ls,
):
    row = lax.axis_index("row")
    col = lax.axis_index("col")
    xh, z = row // 4, row % 4
    xl, y, c = col // 8, (col // 2) % 4, col % 2
    piece = col % 8

    def at(xh_=xh, xl_=xl, y_=y, z_=z, c_=c):
        return (xh_ * 4 + z_, (xl_ * 4 + y_) * 2 + c_)

    zp, zm, z2 = (z + 1) % 4, (z + 3) % 4, (z + 2) % 4
    yp, ym, y2 = (y + 1) % 4, (y + 3) % 4, (y + 2) % 4
    ox, ol, oc = 1 - xh, 1 - xl, 1 - c

    group1 = [
        ((xl + a) % 2, (y + b) % 4, (c + e) % 2)
        for b in (2, 1, 3, 0) for a in (1, 0) for e in range(2) if (a, b, e) != (0, 0, 0)
    ]
    crosses = [((xh + a) % 2, (xl + b) % 2) for a, b in ((1, 0), (1, 1), (0, 1))]
    partners = [at(xl_=a, y_=b, c_=e) for a, b, e in group1]
    partners += [at(xh_=a, z_=b) for a, b in ((xh, zp), (xh, zm), (ox, z), (xh, z2), (ox, zp), (ox, zm), (ox, z2))]
    partners.append(at(xh_=ox, xl_=ol))

    stage = pltpu.make_async_copy(den, local, ls.at[0])
    stage.start()
    barrier = pltpu.get_barrier_semaphore()
    for dev in partners:
        pl.semaphore_signal(barrier, inc=1, device_id=dev, device_id_type=MESH)
    stage.wait()

    def spread(b, carry):
        for j in range(NB):
            first = (j // 24 * NB + b * 8) * 24 + j % 24
            t2src[pl.ds(first, 8, stride=24), :] = local[pl.ds(pl.multiple_of(b * 8, 8), 8), pl.ds(j * BS, BS)]
        return carry

    lax.fori_loop(0, 6, spread, 0)
    pl.semaphore_wait(barrier, len(partners))

    copies = []

    def send(src, dst, dev):
        i = len(copies)
        copy = pltpu.make_async_remote_copy(
            src_ref=src, dst_ref=dst, send_sem=ss.at[i], recv_sem=rs.at[i], device_id=dev, device_id_type=MESH
        )
        copy.start()
        copies.append(copy)
        return copy

    def part1(h, a, b, e):
        half = a if h == OWN else 1 - a
        first = (half * 4 + b) * 768 + e * 384
        return den.at[pl.ds(pl.multiple_of(a * 24, 8), 24), pl.ds(pl.multiple_of(first, 128), 384)]

    def lines(n):
        return pl.ds(pl.multiple_of(n * 144, 8), 144)

    def part2(a, b, e):
        return t2src.at[lines(b * 8 + a * 4 + e)]

    def mid2(a, b, e):
        return t2mid.at[lines((a * 2 + b) * 4 + e)]

    own1, a1 = [None, None], [None, None]

    def deal1(h):
        own1[h] = pltpu.make_async_copy(part1(h, xl, y, c), t1recv.at[h, col], ls.at[1 + h])
        own1[h].start()
        a1[h] = [send(part1(h, a, b, e), t1recv.at[h, col], at(xl_=a, y_=b, c_=e)) for a, b, e in group1]

    a2, b2, own2 = [], [], []

    def deal2():
        for a in range(2):
            for b in range(2):
                copy = pltpu.make_async_copy(part2(a, b, z), mid2(a, b, z), ls.at[3 + a * 2 + b])
                copy.start()
                own2.append(copy)
                for e in (z2, zp, zm):
                    a2.append(send(part2(a, b, e), mid2(a, b, z), at(z_=e)))

    def cross2():
        for copy in own2:
            copy.wait()
        for copy in a2:
            copy.wait_recv()
        own2.clear()
        for n in range(4):
            there = lines((xh * 4 + n) * 2 + xl)
            copy = pltpu.make_async_copy(mid2(xh, xl, n), t2recv.at[there], ls.at[7 + n])
            copy.start()
            own2.append(copy)
            for a, b in crosses:
                b2.append(send(mid2(a, b, n), t2recv.at[there], at(xh_=a, xl_=b)))

    def arrive1(h):
        own1[h].wait()
        for copy in a1[h]:
            copy.wait_recv()
        for j in range(3):
            flat[pl.ds(j * 384, 384), :] = t1recv[h, :, :, pl.ds(j * BS, BS)].reshape(384, BS)
        block = ((xl if h == OWN else ol) * 4 + y) * 6 + c * 3

        def body(b, carry):
            for j in range(3):
                keep = mask_in[xl * 24 + b, block + j].astype(F32)
                for g in range(2):
                    got = flat[pl.ds(j * 384 + g * 192 + b, 8, stride=24), :] * keep
                    acol[b, row, pl.ds(g * 8, 8), pl.ds(h * 384 + j * BS, BS)] = got
            return carry

        lax.fori_loop(0, 24, body, 0)

    def arrive2():
        for copy in own2:
            copy.wait()
        for copy in b2:
            copy.wait_recv()

        def body(b, carry):
            for j in range(24):
                keep = mask_in[row * 6 + b, xl * 24 + j].astype(F32)
                for g in range(2):
                    got = t2recv[pl.ds(g * 8 * 144 + b * 24 + j, 8, stride=144), :] * keep
                    lhs[piece, pl.ds(pl.multiple_of(b * 16 + g * 8, 8), 8), pl.ds(j * BS, BS)] = got
            return carry

        lax.fori_loop(0, 6, body, 0)

    g1 = [{} for _ in CHUNKS]

    def cols(n, slot, part=None):
        h, k, _ = CHUNKS[n]
        first, count = (k * 12, 12) if part is None else (k * 12 + part * 6, 6)
        return acol.at[pl.ds(first, count), slot, :, pl.ds(h * 384, 384)]

    def pass1(n, key, ref, dev):
        g1[n][key] = send(ref, ref, dev)

    def start1(n):
        pass1(n, "x", cols(n, row), at(xh_=ox))
        pass1(n, "zp", cols(n, row), at(z_=zp))
        pass1(n, "zm", cols(n, row), at(z_=zm))

    def relay1(n):
        g1[n]["x"].wait_recv()
        pass1(n, "qp", cols(n, ox * 4 + z), at(z_=zp))
        pass1(n, "qm", cols(n, ox * 4 + z), at(z_=zm))
        g1[n]["zp"].wait_recv()
        pass1(n, "hp", cols(n, xh * 4 + zm, 0), at(z_=zp))
        g1[n]["zm"].wait_recv()
        pass1(n, "hm", cols(n, xh * 4 + zp, 1), at(z_=zm))

    def cross1(n):
        if CHUNKS[n][2] == "x":
            g1[n]["hp"].wait_recv()
            pass1(n, "fp", cols(n, xh * 4 + z2, 0), at(xh_=ox))
            g1[n]["hm"].wait_recv()
            pass1(n, "fm", cols(n, xh * 4 + z2, 1), at(xh_=ox))
        else:
            g1[n]["qp"].wait_recv()
            pass1(n, "fp", cols(n, ox * 4 + zm, 0), at(z_=zp))
            g1[n]["qm"].wait_recv()
            pass1(n, "fm", cols(n, ox * 4 + zp, 1), at(z_=zm))

    def end1(n):
        for key in ("qp", "qm") if CHUNKS[n][2] == "x" else ("hp", "hm"):
            g1[n][key].wait_recv()
        for key in ("fp", "fm"):
            g1[n][key].wait_recv()
        h, k, _ = CHUNKS[n]
        lanes = pl.ds(h * 384, 384)

        def body(b, carry):
            hi, lo = split(acol[b, :, :, lanes].reshape(BS, 384))
            at_ = pl.ds(pl.multiple_of(b * BS, BS), BS)
            bhi[at_, lanes] = hi
            blo[at_, lanes] = lo
            return carry

        lax.fori_loop(k * 12, k * 12 + 12, body, 0)

    g2 = [{}, {}]

    def rows(n, slot, part=None):
        where = slice(None) if part is None else pl.ds(part * 48, 48)
        return lhs.at[slot, where, pl.ds(n * 1536, 1536)]

    def pass2(n, key, ref, dev):
        g2[n][key] = send(ref, ref, dev)

    def start2(n):
        pass2(n, "yp", rows(n, piece), at(y_=yp))
        pass2(n, "ym", rows(n, piece), at(y_=ym))
        pass2(n, "c", rows(n, piece), at(c_=oc))

    def relay2(n):
        g2[n]["yp"].wait_recv()
        pass2(n, "hp", rows(n, ym * 2 + c, 0), at(y_=yp))
        pass2(n, "cyp", rows(n, ym * 2 + c), at(c_=oc))
        g2[n]["ym"].wait_recv()
        pass2(n, "hm", rows(n, yp * 2 + c, 1), at(y_=ym))
        pass2(n, "cym", rows(n, yp * 2 + c), at(c_=oc))

    def far2(n):
        g2[n]["hp"].wait_recv()
        pass2(n, "chp", rows(n, y2 * 2 + c, 0), at(c_=oc))
        g2[n]["hm"].wait_recv()
        pass2(n, "chm", rows(n, y2 * 2 + c, 1), at(c_=oc))

    def end2(n):
        for key in ("c", "cyp", "cym", "chp", "chm"):
            g2[n][key].wait_recv()

    s1 = []

    def other(there):
        m = pl.ds(there * 192, 192)
        lanes = pl.ds(384, 384)
        for n in range(2):
            k = pl.ds(n * 1536, 1536)
            got = dot3(lhs[pl.ds(there * 2, 2), :, k].reshape(192, 1536), bhi[k, lanes], blo[k, lanes])
            so[m, :] = got if n == 0 else so[m, :] + got
        s1.append(send(so.at[m], rs1.at[m], at(xl_=ol)))

    def own_rows(r, n):
        k = pl.ds(n * 1536, 1536)
        a = lhs[pl.ds(r * PIECES, PIECES), :, k].reshape(ROWS, 1536)
        return dot3(a, bhi[k, pl.ds(0, 384)], blo[k, pl.ds(0, 384)])

    deal1(OTHER)
    deal2()
    arrive1(OTHER)
    start1(0)
    start1(1)
    deal1(OWN)
    cross2()
    relay1(0)
    arrive1(OWN)
    arrive2()
    start2(0)
    start2(1)
    relay1(1)
    start1(2)
    cross1(0)
    relay2(0)
    relay1(2)
    start1(3)
    cross1(1)
    end1(0)
    relay2(1)
    far2(0)
    end1(1)
    cross1(2)
    far2(1)
    end2(0)
    end2(1)
    other(0)
    relay1(3)
    other(1)
    end1(2)
    other(2)
    other(3)

    def first_half(i, carry):
        m = pl.ds(pl.multiple_of(i * 192, 64), 192)
        k = pl.ds(0, 1536)
        a = lhs[pl.ds(i * 2, 2), :, k].reshape(192, 1536)
        sw[m, :] = dot3(a, bhi[k, pl.ds(0, 384)], blo[k, pl.ds(0, 384)])
        return carry

    lax.fori_loop(0, 2, first_half, 0)
    cross1(3)
    lax.fori_loop(2, 4, first_half, 0)
    end1(3)

    mine = pl.multiple_of(piece * 384, 128)
    block = col * 3
    keep_sq = [[mask_sq[row * 6 + b, block + j].astype(F32) for j in range(3)] for b in range(6)]
    keep_cube = [[mask_cube[row * 6 + b, block + j].astype(F32) for j in range(3)] for b in range(6)]
    diag_sq = [3.0 * mask_sq[row * 6 + b, row * 6 + b].astype(F32) for b in range(6)]
    diag_cube = [2.0 * mask_cube[row * 6 + b, row * 6 + b].astype(F32) for b in range(6)]
    g3 = [{} for _ in range(RC)]
    s2 = [None] * RC

    def pass3(r, key, ref, dev):
        g3[r][key] = send(ref, ref, dev)

    def begin3(r):
        m = pl.ds(r * ROWS, ROWS)
        got = own_rows(r, 1) + sw[m, :]
        if r % (RC // 4) == 0:
            s1[r * 4 // RC].wait_recv()
        got = got + rs1[m, :]
        total = jnp.zeros((8, BS), F32)
        for i in range(PIECES):
            for b in range(6):
                for j in range(3):
                    first, lanes = i * 96 + b * 16, pl.ds(j * BS, BS)
                    s = got[first:first + 16, j * BS:(j + 1) * BS] * keep_sq[b][j]
                    sfull[piece, pl.ds(r * ROWS + first, 16), lanes] = s
                    a = lhs[r * PIECES + i, pl.ds(b * 16, 16), pl.ds(pl.multiple_of(mine + j * BS, BS), BS)]
                    part = a * (a * diag_sq[b] - s * diag_cube[b])
                    total = total + part[0:8] + part[8:16]
        tacc[...] = total if r == 0 else tacc[...] + total
        ref = sfull.at[piece, m]
        pass3(r, "yp", ref, at(y_=yp))
        pass3(r, "ym", ref, at(y_=ym))
        pass3(r, "c", ref, at(c_=oc))

    def square(r, slot, part=None):
        first, count = (r * ROWS, ROWS) if part is None else (r * ROWS + part * (ROWS // 2), ROWS // 2)
        return sfull.at[slot, pl.ds(first, count)]

    def relay3(r):
        g3[r]["yp"].wait_recv()
        pass3(r, "hp", square(r, ym * 2 + c, 0), at(y_=yp))
        pass3(r, "cyp", square(r, ym * 2 + c), at(c_=oc))
        g3[r]["ym"].wait_recv()
        pass3(r, "hm", square(r, yp * 2 + c, 1), at(y_=ym))
        pass3(r, "cym", square(r, yp * 2 + c), at(c_=oc))

    def far3(r):
        g3[r]["hp"].wait_recv()
        pass3(r, "chp", square(r, y2 * 2 + c, 0), at(c_=oc))
        g3[r]["hm"].wait_recv()
        pass3(r, "chm", square(r, y2 * 2 + c, 1), at(c_=oc))

    def cube(r):
        m = pl.ds(r * ROWS, ROWS)
        for key in ("c", "cyp", "cym", "chp", "chm"):
            g3[r][key].wait_recv()

        def body(s, carry):
            k = pl.ds(pl.multiple_of(s * 384, 384), 384)
            cacc[m, :] = cacc[m, :] + dot3(sfull[s, m, :], bhi[k, :], blo[k, :])
            return carry

        cacc[m, :] = jnp.zeros((ROWS, 768), F32)
        lax.fori_loop(0, 8, body, 0)
        s2[r] = send(cacc.at[m, pl.ds(384, 384)], rs2.at[m], at(xl_=ol))

    def finish(r):
        m = pl.ds(r * ROWS, ROWS)
        s2[r].wait_recv()
        got = cacc[m, pl.ds(0, 384)] + rs2[m, :]
        for i in range(PIECES):
            for j in range(3):
                parts = []
                for b in range(6):
                    first = i * 96 + b * 16
                    parts.append(got[first:first + 16, j * BS:(j + 1) * BS] * (2.0 * keep_cube[b][j]))
                s = sfull[piece, pl.ds(r * ROWS + i * 96, 96), pl.ds(j * BS, BS)]
                flat2 = 3.0 * s - jnp.concatenate(parts, axis=0)
                t2recv[pl.ds(j * 768 + r * PIECES + i, 96, stride=8), :] = flat2

    across = [at(xl_=a, y_=b, c_=e) for a, b, e in group1]
    along = [at(xh_=a, z_=b) for a, b in ((xh, zp), (xh, zm), (ox, z), (xh, z2), (ox, zp), (ox, zm), (ox, z2))]
    sums = []

    def trace_first():
        tone[col] = tacc[...]
        sums.append([send(tone.at[col], tone.at[col], dev) for dev in across])

    def trace_second():
        for copy in sums[0]:
            copy.wait_recv()
        ttwo[row] = jnp.sum(tone[...], axis=0)
        sums.append([send(ttwo.at[row], ttwo.at[row], dev) for dev in along])

    def trace_third():
        for copy in sums[1]:
            copy.wait_recv()
        trace[0, 0] = jnp.sum(ttwo[...])

    begin3(0)
    begin3(1)
    for t in range(RC + 3):
        if t < RC:
            relay3(t)
        if t + 2 < RC:
            begin3(t + 2)
        if 0 <= t - 1 < RC:
            far3(t - 1)
        if t == RC - 2:
            trace_first()
        if 0 <= t - 2 < RC:
            cube(t - 2)
        if t == RC + 1:
            trace_second()
        if 0 <= t - 3 < RC:
            finish(t - 3)
    for j in range(3):
        out[:, pl.ds(j * BS, BS)] = t2recv[pl.ds(j * 768, 768), :]
    trace_third()
    assert len(copies) == N_COPIES
    for copy in copies:
        copy.wait_send()


N_COPIES = 54 + 9 * len(CHUNKS) + 2 * 9 + 4 + RC * 10 + 22


def call(den, mask_in, mask_sq, mask_cube):
    vmem = pl.BlockSpec(memory_space=pltpu.VMEM)
    smem = pl.BlockSpec(memory_space=pltpu.SMEM)
    return pl.pallas_call(
        kernel,
        out_shape=(jax.ShapeDtypeStruct((768, 384), F32), jax.ShapeDtypeStruct((1, 1), F32)),
        in_specs=[pl.BlockSpec(memory_space=pl.ANY), smem, smem, smem],
        out_specs=(vmem, smem),
        scratch_shapes=[
            pltpu.VMEM((NB, 6144), F32),
            pltpu.VMEM((2, 16, 24, 384), F32),
            pltpu.VMEM((2304, BS), F32),
            pltpu.VMEM((2304, BS), F32),
            pltpu.VMEM((2304, BS), F32),
            pltpu.VMEM((1152, BS), F32),
            pltpu.VMEM((24, 8, 16, 768), F32),
            pltpu.VMEM((8, 96, HALF), F32),
            pltpu.VMEM((HALF, 768), BF16),
            pltpu.VMEM((HALF, 768), BF16),
            pltpu.VMEM((768, 384), F32),
            pltpu.VMEM((768, 384), F32),
            pltpu.VMEM((768, 384), F32),
            pltpu.VMEM((8, 768, 384), F32),
            pltpu.VMEM((768, 768), F32),
            pltpu.VMEM((768, 384), F32),
            pltpu.VMEM((8, BS), F32),
            pltpu.VMEM((16, 8, BS), F32),
            pltpu.VMEM((8, 8, BS), F32),
            pltpu.SemaphoreType.DMA((N_COPIES,)),
            pltpu.SemaphoreType.DMA((N_COPIES,)),
            pltpu.SemaphoreType.DMA((11,)),
        ],
        compiler_params=pltpu.CompilerParams(
            collective_id=0, has_side_effects=True, vmem_limit_bytes=62 * 2**20
        ),
        cost_estimate=pl.CostEstimate(flops=2 * 768 * 768 * HALF * 6, bytes_accessed=4 * 2**20, transcendentals=0),
    )(den, mask_in, mask_sq, mask_cube)


def shards(density_cyclic, mask_in, mask_sq, mask_cube):
    purified, trace = call(density_cyclic, mask_in, mask_sq, mask_cube)
    return purified, trace[0, 0]


def solution(mesh):
    in_specs = (P(("row", "col"), None), P(), P(), P())
    out_specs = (P("row", "col"), P())
    return jax.shard_map(shards, mesh=mesh, in_specs=in_specs, out_specs=out_specs, check_vma=False)
```

time: 507 us -> 181 us (0.36)
  waiting for transfers between devices: 335 us -> 0 us
  Pallas kernels: 0 us -> 176 us
  matrix products: 69.2 us -> 0 us
  blocking collectives: 65.4 us -> 0 us
  between operations: 13.9 us -> 2.39 us
  starting transfers between devices: 10.6 us -> 0 us
  local copies, waits for them, and re-layouts: 8.61 us -> 2.36 us
    all_gather x3 -> x0, waiting for transfers between devices: 314 us -> none  [the longest x1 111 us: shards(): lax.all_gather(filtered, 'row', axis=0, tiled=True)]
    pallas_call x0 -> x1, Pallas kernels: none -> 176 us  [call(): pl.pallas_call(kernel, out_shape=(jax.ShapeDtypeStruct((768, 384), F32),...]
    dot_general x2 -> x0, matrix products: 69.2 us -> none  [fold_rows(): jnp.dot(panel, piece, precision=lax.Precision.HIGHEST, preferred_element_...]
    psum x1 -> x0, blocking collectives: 65.4 us -> none  [shards(): total = lax.psum(partial_trace, ('row', 'col'))]
    all_to_all x1 -> x0, waiting for transfers between devices: 20.2 us -> none  [shards(): lax.all_to_all(outgoing, ('row', 'col'), split_axis=0, concat_axis=0, til...]
    all_to_all x1 -> x0, starting transfers between devices: 10.4 us -> none  [shards(): lax.all_to_all(outgoing, ('row', 'col'), split_axis=0, concat_axis=0, til...]
  transfers between devices with their start and end apart: 4 -> 0, of which waited for: 4 -> 0; matrix products, arithmetic and copies ran while one was open for 1% -> 0% of each run, Pallas kernels for 0% -> 0%
where the time goes in v2:
time: 181 us; the launch traced here: 180 us
  Pallas kernels  176 us (97%)
  between operations  2.39 us (1%)
  local copies, waits for them, and re-layouts  2.36 us (1%)
    pallas_call x1, Pallas kernels, call(): pl.pallas_call(kernel, out_shape=(jax.ShapeDtypeStruct((768, 384), F32),...  176 us

profile of v2, /device:TPU:8, one launch (start us, length us, event | category | flops | bytes accessed | tf_op | source)
XLA Modules:
  0.0 180.5 jit_solution(3746717238092096398)
XLA Ops:
  0.6 175.7 %shard_map.59 = (f32[768,384]{1,0:T(8,128)}, f32[1,1]{1,0:T(1,128)}) custom-call(f32[48,6144]{1,0:T(8,128)} %den.1, s32[48,48]{1,0:T(8,128)} %mask_in.1, s32[48,48]{1,0:T(8,128)} %mask_sq.1, s32[48,48]{1,0:T(8,128)} %mask_cube.1), custom_call_target="tpu_custom_call" | custom-call | flops 21743271936 | bytes 4194304 | tf_op jit(solution)/shard_map/pallas_call | solution.py:446
  176.4 2.4 %copy.8 = f32[768,384]{1,0:T(8,128)} copy(f32[768,384]{1,0:T(8,128)} %get-tuple-element.8) | data formatting | bytes 2359296

commit v3 on v2

--- a/solution.py
+++ b/solution.py
@@ -29,12 +29,14 @@
 
 def dot3(a, bh, bl):
     ah, al = split(a)
-    return dot(ah, bh) + (dot(al, bh) + dot(ah, bl))
+    n = a.shape[0]
+    both = dot(jnp.concatenate([ah, al], axis=0), bh)
+    return both[:n] + (both[n:] + dot(ah, bl))
 
 
 def kernel(
     den, mask_in, mask_sq, mask_cube, out, trace,
-    local, t1recv, t2src, t2mid, t2recv, flat, acol, lhs, bhi, blo, so, sw, rs1, sfull, cacc, rs2, tacc, tone, ttwo,
+    local, t1recv, t2src, t2recv, flat, acol, lhs, bhi, blo, so, sw, rs1, sfull, cacc, rs2, tacc, tone, ttwo,
     ss, rs, ls,
 ):
     row = lax.axis_index("row")
@@ -54,10 +56,12 @@
         ((xl + a) % 2, (y + b) % 4, (c + e) % 2)
         for b in (2, 1, 3, 0) for a in (1, 0) for e in range(2) if (a, b, e) != (0, 0, 0)
     ]
-    crosses = [((xh + a) % 2, (xl + b) % 2) for a, b in ((1, 0), (1, 1), (0, 1))]
+    group2 = [
+        ((xh + a) % 2, (xl + b) % 2, (z + e) % 4)
+        for e in (2, 1, 3, 0) for a in (1, 0) for b in (1, 0) if (a, b, e) != (0, 0, 0)
+    ]
     partners = [at(xl_=a, y_=b, c_=e) for a, b, e in group1]
-    partners += [at(xh_=a, z_=b) for a, b in ((xh, zp), (xh, zm), (ox, z), (xh, z2), (ox, zp), (ox, zm), (ox, z2))]
-    partners.append(at(xh_=ox, xl_=ol))
+    partners += [at(xh_=a, xl_=b, z_=e) for a, b, e in group2[:-1]]
 
     stage = pltpu.make_async_copy(den, local, ls.at[0])
     stage.start()
@@ -97,9 +101,6 @@
     def part2(a, b, e):
         return t2src.at[lines(b * 8 + a * 4 + e)]
 
-    def mid2(a, b, e):
-        return t2mid.at[lines((a * 2 + b) * 4 + e)]
-
     own1, a1 = [None, None], [None, None]
 
     def deal1(h):
@@ -107,30 +108,14 @@
         own1[h].start()
         a1[h] = [send(part1(h, a, b, e), t1recv.at[h, col], at(xl_=a, y_=b, c_=e)) for a, b, e in group1]
 
-    a2, b2, own2 = [], [], []
+    a2, own2 = [], []
 
     def deal2():
-        for a in range(2):
-            for b in range(2):
-                copy = pltpu.make_async_copy(part2(a, b, z), mid2(a, b, z), ls.at[3 + a * 2 + b])
-                copy.start()
-                own2.append(copy)
-                for e in (z2, zp, zm):
-                    a2.append(send(part2(a, b, e), mid2(a, b, z), at(z_=e)))
-
-    def cross2():
-        for copy in own2:
-            copy.wait()
-        for copy in a2:
-            copy.wait_recv()
-        own2.clear()
-        for n in range(4):
-            there = lines((xh * 4 + n) * 2 + xl)
-            copy = pltpu.make_async_copy(mid2(xh, xl, n), t2recv.at[there], ls.at[7 + n])
-            copy.start()
-            own2.append(copy)
-            for a, b in crosses:
-                b2.append(send(mid2(a, b, n), t2recv.at[there], at(xh_=a, xl_=b)))
+        there = lines(row * 2 + xl)
+        own2.append(pltpu.make_async_copy(part2(xh, xl, z), t2recv.at[there], ls.at[3]))
+        own2[0].start()
+        for a, b, e in group2:
+            a2.append(send(part2(a, b, e), t2recv.at[there], at(xh_=a, xl_=b, z_=e)))
 
     def arrive1(h):
         own1[h].wait()
@@ -153,7 +138,7 @@
     def arrive2():
         for copy in own2:
             copy.wait()
-        for copy in b2:
+        for copy in a2:
             copy.wait_recv()
 
         def body(b, carry):
@@ -273,7 +258,6 @@
     start1(0)
     start1(1)
     deal1(OWN)
-    cross2()
     relay1(0)
     arrive1(OWN)
     arrive2()
@@ -291,15 +275,16 @@
     far2(0)
     end1(1)
     cross1(2)
+    relay1(3)
     far2(1)
+    cross1(3)
     end2(0)
     end2(1)
     other(0)
-    relay1(3)
     other(1)
-    end1(2)
     other(2)
     other(3)
+    end1(2)
 
     def first_half(i, carry):
         m = pl.ds(pl.multiple_of(i * 192, 64), 192)
@@ -308,9 +293,7 @@
         sw[m, :] = dot3(a, bhi[k, pl.ds(0, 384)], blo[k, pl.ds(0, 384)])
         return carry
 
-    lax.fori_loop(0, 2, first_half, 0)
-    cross1(3)
-    lax.fori_loop(2, 4, first_half, 0)
+    lax.fori_loop(0, 4, first_half, 0)
     end1(3)
 
     mine = pl.multiple_of(piece * 384, 128)
@@ -354,29 +337,31 @@
     def relay3(r):
         g3[r]["yp"].wait_recv()
         pass3(r, "hp", square(r, ym * 2 + c, 0), at(y_=yp))
-        pass3(r, "cyp", square(r, ym * 2 + c), at(c_=oc))
         g3[r]["ym"].wait_recv()
         pass3(r, "hm", square(r, yp * 2 + c, 1), at(y_=ym))
+        pass3(r, "cyp", square(r, ym * 2 + c), at(c_=oc))
         pass3(r, "cym", square(r, yp * 2 + c), at(c_=oc))
 
     def far3(r):
         g3[r]["hp"].wait_recv()
-        pass3(r, "chp", square(r, y2 * 2 + c, 0), at(c_=oc))
         g3[r]["hm"].wait_recv()
-        pass3(r, "chm", square(r, y2 * 2 + c, 1), at(c_=oc))
+        pass3(r, "cfar", square(r, y2 * 2 + c), at(c_=oc))
 
     def cube(r):
         m = pl.ds(r * ROWS, ROWS)
-        for key in ("c", "cyp", "cym", "chp", "chm"):
+        for key in ("c", "cyp", "cym", "cfar"):
             g3[r][key].wait_recv()
 
-        def body(s, carry):
-            k = pl.ds(pl.multiple_of(s * 384, 384), 384)
-            cacc[m, :] = cacc[m, :] + dot3(sfull[s, m, :], bhi[k, :], blo[k, :])
+        def body(h, carry):
+            lanes = pl.ds(pl.multiple_of(384 - h * 384, 128), 384)
+            acc = jnp.zeros((ROWS, 384), F32)
+            for s in range(8):
+                k = pl.ds(s * 384, 384)
+                acc = acc + dot3(sfull[s, m, :], bhi[k, lanes], blo[k, lanes])
+            cacc[m, lanes] = acc
             return carry
 
-        cacc[m, :] = jnp.zeros((ROWS, 768), F32)
-        lax.fori_loop(0, 8, body, 0)
+        lax.fori_loop(0, 2, body, 0)
         s2[r] = send(cacc.at[m, pl.ds(384, 384)], rs2.at[m], at(xl_=ol))
 
     def finish(r):
@@ -437,7 +422,7 @@
         copy.wait_send()
 
 
-N_COPIES = 54 + 9 * len(CHUNKS) + 2 * 9 + 4 + RC * 10 + 22
+N_COPIES = 45 + 9 * len(CHUNKS) + 2 * 9 + 4 + RC * 9 + 22
 
 
 def call(den, mask_in, mask_sq, mask_cube):
@@ -451,7 +436,6 @@
         scratch_shapes=[
             pltpu.VMEM((NB, 6144), F32),
             pltpu.VMEM((2, 16, 24, 384), F32),
-            pltpu.VMEM((2304, BS), F32),
             pltpu.VMEM((2304, BS), F32),
             pltpu.VMEM((2304, BS), F32),
             pltpu.VMEM((1152, BS), F32),
@@ -470,7 +454,7 @@
             pltpu.VMEM((8, 8, BS), F32),
             pltpu.SemaphoreType.DMA((N_COPIES,)),
             pltpu.SemaphoreType.DMA((N_COPIES,)),
-            pltpu.SemaphoreType.DMA((11,)),
+            pltpu.SemaphoreType.DMA((4,)),
         ],
         compiler_params=pltpu.CompilerParams(
             collective_id=0, has_side_effects=True, vmem_limit_bytes=62 * 2**20

time: 181 us -> 176 us (0.972)
  Pallas kernels: 176 us -> 171 us
    pallas_call x1, Pallas kernels: 176 us -> 171 us  [call(): pl.pallas_call(kernel, out_shape=(jax.ShapeDtypeStruct((768, 384), F32),...]
where the time goes in v3:
time: 176 us; the launch traced here: 175 us
  Pallas kernels  171 us (97%)
  between operations  2.39 us (1%)
  local copies, waits for them, and re-layouts  2.36 us (1%)
    pallas_call x1, Pallas kernels, call(): pl.pallas_call(kernel, out_shape=(jax.ShapeDtypeStruct((768, 384), F32),...  171 us

profile of v3, /device:TPU:8, one launch (start us, length us, event | category | flops | bytes accessed | tf_op | source)
XLA Modules:
  0.0 175.4 jit_solution(2598290273707485441)
XLA Ops:
  0.6 170.6 %shard_map.59 = (f32[768,384]{1,0:T(8,128)}, f32[1,1]{1,0:T(1,128)}) custom-call(f32[48,6144]{1,0:T(8,128)} %den.1, s32[48,48]{1,0:T(8,128)} %mask_in.1, s32[48,48]{1,0:T(8,128)} %mask_sq.1, s32[48,48]{1,0:T(8,128)} %mask_cube.1), custom_call_target="tpu_custom_call" | custom-call | flops 21743271936 | bytes 4194304 | tf_op jit(solution)/shard_map/pallas_call | solution.py:431
  171.3 2.4 %copy.8 = f32[768,384]{1,0:T(8,128)} copy(f32[768,384]{1,0:T(8,128)} %get-tuple-element.8) | data formatting | bytes 2359296

commit v4 on v3

--- a/solution.py
+++ b/solution.py
@@ -221,9 +221,9 @@
     def relay2(n):
         g2[n]["yp"].wait_recv()
         pass2(n, "hp", rows(n, ym * 2 + c, 0), at(y_=yp))
-        pass2(n, "cyp", rows(n, ym * 2 + c), at(c_=oc))
         g2[n]["ym"].wait_recv()
         pass2(n, "hm", rows(n, yp * 2 + c, 1), at(y_=ym))
+        pass2(n, "cyp", rows(n, ym * 2 + c), at(c_=oc))
         pass2(n, "cym", rows(n, yp * 2 + c), at(c_=oc))
 
     def far2(n):
@@ -277,10 +277,10 @@
     cross1(2)
     relay1(3)
     far2(1)
-    cross1(3)
     end2(0)
     end2(1)
     other(0)
+    cross1(3)
     other(1)
     other(2)
     other(3)

time: 176 us -> 174 us (0.989)
  Pallas kernels: 171 us -> 169 us
    pallas_call x1, Pallas kernels: 171 us -> 169 us  [call(): pl.pallas_call(kernel, out_shape=(jax.ShapeDtypeStruct((768, 384), F32),...]
where the time goes in v4:
time: 174 us; the launch traced here: 173 us
  Pallas kernels  169 us (97%)
  between operations  2.39 us (1%)
  local copies, waits for them, and re-layouts  2.36 us (1%)
    pallas_call x1, Pallas kernels, call(): pl.pallas_call(kernel, out_shape=(jax.ShapeDtypeStruct((768, 384), F32),...  169 us

profile of v4, /device:TPU:8, one launch (start us, length us, event | category | flops | bytes accessed | tf_op | source)
XLA Modules:
  0.0 173.4 jit_solution(3603279563139185967)
XLA Ops:
  0.6 168.6 %shard_map.59 = (f32[768,384]{1,0:T(8,128)}, f32[1,1]{1,0:T(1,128)}) custom-call(f32[48,6144]{1,0:T(8,128)} %den.1, s32[48,48]{1,0:T(8,128)} %mask_in.1, s32[48,48]{1,0:T(8,128)} %mask_sq.1, s32[48,48]{1,0:T(8,128)} %mask_cube.1), custom_call_target="tpu_custom_call" | custom-call | flops 21743271936 | bytes 4194304 | tf_op jit(solution)/shard_map/pallas_call | solution.py:431
  169.2 2.4 %copy.8 = f32[768,384]{1,0:T(8,128)} copy(f32[768,384]{1,0:T(8,128)} %get-tuple-element.8) | data formatting | bytes 2359296
